TPU v7x, 512 devices: a whole 4x8x8 slice. The times are simulated.
512 devices in a mesh: dp: 16 (over z, core), tensor: 32 (over x, y).
Axes of the slice: x: 4, y: 8, z: 8, core: 2. Of those that a mesh axis runs over, the one named last changes fastest.
Arguments:
- activations: bfloat16 [12288, 4096], P('dp', 'tensor'), may hold values from -6 to 6
- out_grads_t: bfloat16 [5504, 12288], P('tensor', 'dp'), may hold values from -6 to 6
- in_basis: bfloat16 [4096, 4096], P(None, 'tensor'), may hold values from -0.09375 to 0.09375
- out_basis_t: bfloat16 [5504, 5504], P('tensor'), may hold values from -0.078125 to 0.078125
- query_proj: bfloat16 [4, 5504, 4096], P(None, 'tensor', 'dp'), may hold values from -6 to 6
- eigvals: float32 [5504, 4096], P('tensor', 'dp'), may hold values from 0.05 to 5
- damping: float32 [1], replicated, may hold values from 0.05 to 0.2
- lengths: int32 [96], P('dp'), may hold values from 1 to 128, 7680 in all
Outputs:
- scores: float32 [96, 4], P('dp')
Inputs may be any that keep to these rules, and one draw needn't show every extreme that they name: `lengths`: the largest token count is exactly 128.
All inputs are finite; a program needn't handle non-finite values. No bound on the sum of `lengths` on one device may be relied on, other than what follows from the above.
Results may differ from a plain program's by a relative error of at most 0.006.
Values may be sent and summed in bfloat16 or wider, within the bound.
No kernel may reach another device: no remote copies, remote signals or barrier semaphores. Data moves between devices by JAX's collectives and lax.ppermute only.
A program may use at most 128 MiB of HBM per device.

v0:
```python
import jax
import jax.numpy as jnp
from jax import lax
from jax.sharding import PartitionSpec as P


def local(activations, out_grads_t, in_basis, out_basis_t, query_proj, eigvals, damping, lengths):
    full_act = lax.all_gather(activations, "tensor", axis=1, tiled=True)
    act_local = jnp.dot(full_act, in_basis, preferred_element_type=jnp.float32).astype(jnp.bfloat16)
    act_proj = lax.all_gather(act_local, "tensor", axis=1, tiled=True)
    token_rows = full_act.shape[0]
    width = out_basis_t.shape[0]
    grad_full = jnp.dot(
        out_basis_t,
        lax.all_gather(out_grads_t, "tensor", axis=0, tiled=True),
        preferred_element_type=jnp.float32,
    )
    seq_count = lengths.shape[0]
    seq_len = token_rows // seq_count
    position = lax.broadcasted_iota(jnp.int32, (seq_count, seq_len), 1)
    keep = (position < lengths[:, None]).astype(jnp.float32).reshape(1, token_rows)
    grad_proj = (grad_full * keep).astype(jnp.bfloat16)
    scaled = (query_proj.astype(jnp.float32) / (eigvals + damping[0])).astype(jnp.bfloat16)
    projected = jnp.einsum(
        "jst,std->sjd",
        grad_proj.reshape(width, seq_count, seq_len),
        act_proj.reshape(seq_count, seq_len, act_proj.shape[1]),
        preferred_element_type=jnp.float32,
    )
    partial_value = jnp.einsum(
        "sij,qij->sq",
        projected,
        lax.all_gather(scaled, "dp", axis=2, tiled=True).astype(jnp.float32),
    )
    totals = lax.psum(partial_value, "tensor")
    norm_factor = (act_proj.shape[1] * out_basis_t.shape[1] * seq_len) ** (-0.5)
    return totals * norm_factor


def solution(mesh):
    placed = (
        P("dp", "tensor"),
        P("tensor", "dp"),
        P(None, "tensor"),
        P("tensor", None),
        P(None, "tensor", "dp"),
        P("tensor", "dp"),
        P(),
        P("dp"),
    )
    return jax.shard_map(
        local, mesh=mesh, in_specs=placed, out_specs=P("dp", None), check_vma=False
    )
```

profile of v0, /device:TPU:64, one launch (start us, length us, event | category | flops | bytes accessed | tf_op | source)
XLA Modules:
  0.0 474.7 jit_solution(10755105774203012612)
XLA Ops:
  6.5 0.0 copy-start
  6.5 0.0 copy-start.2
  6.5 0.0 copy-start.1
  6.5 0.0 copy-start.3
  6.5 0.0 all-gather.6.cloned.1.call-start
  6.6 0.7 all-gather.6.cloned.1.call-update
  7.3 0.0 all-gather.12.cloned.1.call-start
  7.3 0.7 all-gather.12.cloned.1.call-update
  8.0 0.0 all-gather.8.cloned.1.call-start
  8.1 104.2 %all-gather.6.cloned.1.call-done = bf16[768,4096]{1,0:T(8,128)(2,1)} async-done(((bf16[768,128]{1,0:T(8,128)(2,1)}), bf16[768,4096]{1,0:T(8,128)(2,1)}) %all-gather.6.cloned.1.call-update) | async-done | bytes 6291472 | tf_op jit(solution)/shard_map/all_gather | solution.py:8
  112.3 5.5 %convolution_convert_fusion = bf16[768,128]{1,0:T(8,128)(2,1)} fusion(bf16[768,4096]{1,0:T(8,128)(2,1)} %all-gather.6.cloned.1.call-done, bf16[4096,128]{1,0:T(8,128)(2,1)} %param.10), kind=kOutput, calls=%fused_computation.4 | convolution fusion | flops 805404672 | bytes 7536640 | tf_op jit(solution)/shard_map/dot_general | solution.py:9
  117.8 0.0 all-gather.8.cloned.1.call-update
  117.8 0.0 all-gather.10.cloned.1.call-start
  118.5 0.0 copy-done.2
  118.5 0.0 copy-done.1
  118.5 0.9 fusion.6
  119.5 0.0 all-gather.10.cloned.1.call-update
  119.5 0.0 copy-done.3
  119.5 0.1 convert_bitcast_fusion
  119.6 100.5 %all-gather.12.cloned.1.call-done = bf16[32,172,768]{2,1,0:T(8,128)(2,1)} async-done(((bf16[1,172,768]{2,1,0:T(8,128)(2,1)}), bf16[32,172,768]{2,1,0:T(8,128)(2,1)}) %all-gather.12.cloned.1.call-update) | async-done | bytes 8454160 | tf_op jit(solution)/shard_map/all_gather | solution.py:15
  220.1 12.5 %reshape.30 = bf16[5504,768]{1,0:T(8,128)(2,1)} reshape(bf16[32,172,768]{2,1,0:T(8,128)(2,1)} %all-gather.12.cloned.1.call-done) | data formatting | bytes 16908288
  232.6 0.0 copy-done
  232.6 5.2 %fusion.2 = bf16[172,768]{1,0:T(8,128)(2,1)S(1)} fusion(bf16[172,5504]{1,0:T(8,128)(2,1)S(1)} %copy-done, bf16[5504,768]{1,0:T(8,128)(2,1)} %reshape.30, f32[768]{0:T(1024)S(1)} %convert_bitcast_fusion), kind=kOutput, calls=%fused_computation.3 | convolution fusion | flops 1454376960 | bytes 10614784 | tf_op jit(solution)/shard_map/dot_general | solution.py:13
  237.7 0.3 reshape.26
  238.0 80.5 %all-gather.8.cloned.1.call-done = bf16[768,4096]{1,0:T(8,128)(2,1)} async-done(((bf16[768,128]{1,0:T(8,128)(2,1)}), bf16[768,4096]{1,0:T(8,128)(2,1)}) %all-gather.8.cloned.1.call-update) | async-done | bytes 6291472 | tf_op jit(solution)/shard_map/all_gather | solution.py:10
  318.6 8.5 %fusion.7 = bf16[6,172,4096]{2,1,0:T(8,128)(2,1)} fusion(bf16[6,128,4096]{2,1,0:T(8,128)(2,1)} %bitcast.14, bf16[172,6,128]{2,1,0:T(8,128)(2,1)S(1)} %reshape.26), kind=kOutput, calls=%fused_computation.8 | convolution fusion | flops 1082130432 | bytes 15009792 | tf_op jit(solution)/shard_map/jst,std->sjd/dot_general | solution.py:24
  327.1 51.2 %all-gather.10.cloned.1.call-done = bf16[4,172,4096]{2,0,1:T(4,128)(2,1)} async-done(((bf16[4,172,256]{2,0,1:T(4,128)(2,1)}), bf16[4,172,4096]{2,0,1:T(4,128)(2,1)}) %all-gather.10.cloned.1.call-update) | async-done | bytes 5636112 | tf_op jit(solution)/shard_map/all_gather | solution.py:33
  378.3 15.5 %fusion.3 = f32[6,4]{0,1:T(4,128)S(1)} fusion(bf16[4,172,4096]{2,0,1:T(4,128)(2,1)} %all-gather.10.cloned.1.call-done, bf16[6,172,4096]{2,1,0:T(8,128)(2,1)} %fusion.7), kind=kOutput, calls=%fused_computation.5 | convolution fusion | flops 33816576 | bytes 14090336 | tf_op jit(solution)/shard_map/sij,qij->sq/dot_general | solution.py:30
  393.8 73.8 %psum.7 = f32[6,4]{0,1:T(4,128)S(1)} all-reduce(f32[6,4]{0,1:T(4,128)S(1)} %fusion.3), channel_id=1, replica_groups=mesh['dp'=16,'tensor'=32] {'tensor'}, use_global_device_ids=true, to_apply=%region_0.0 | all-reduce | flops 24 | bytes 192 | tf_op jit(solution)/shard_map/psum | solution.py:35
  467.6 0.6 broadcast_multiply_fusion
  (1 shorter events, 0.0 us)
Async XLA Ops:
  6.5 226.0 %copy-start = (bf16[172,5504]{1,0:T(8,128)(2,1)S(1)}, bf16[172,5504]{1,0:T(8,128)(2,1)}, u32[]{:S(2)}) copy-start(bf16[172,5504]{1,0:T(8,128)(2,1)} %param.11) | copy-start | bytes 5680132
  6.5 111.9 %copy-start.2 = (f32[172,256]{1,0:T(8,128)S(1)}, f32[172,256]{1,0:T(8,128)}, u32[]{:S(2)}) copy-start(f32[172,256]{1,0:T(8,128)} %param.13) | copy-start | bytes 528388
  6.5 112.0 %copy-start.1 = (bf16[4,172,256]{2,0,1:T(4,128)(2,1)S(1)}, bf16[4,172,256]{2,0,1:T(4,128)(2,1)}, u32[]{:S(2)}) copy-start(bf16[4,172,256]{2,0,1:T(4,128)(2,1)} %param.12) | copy-start | bytes 1056772
  6.5 112.9 %copy-start.3 = (s32[6]{0:T(128)S(1)}, s32[6]{0:T(128)}, u32[]{:S(2)}) copy-start(s32[6]{0:T(128)} %param.15) | copy-start | bytes 76
  6.5 105.7 %all-gather.6.cloned.1.call-start = ((), (), s32[]{:S(2)}) async-start(), calls=%async_computation | async-start | bytes 6488064 | tf_op jit(solution)/shard_map/all_gather | solution.py:8
  7.3 212.8 %all-gather.12.cloned.1.call-start = ((), (), s32[]{:S(2)}) async-start(), calls=%async_computation.3 | async-start | bytes 8921088 | tf_op jit(solution)/shard_map/all_gather | solution.py:15
  8.0 310.6 %all-gather.8.cloned.1.call-start = ((), (), s32[]{:S(2)}) async-start(), calls=%async_computation.1 | async-start | bytes 6488064 | tf_op jit(solution)/shard_map/all_gather | solution.py:10
  117.8 260.5 %all-gather.10.cloned.1.call-start = ((), (), s32[]{:S(2)}) async-start(), calls=%async_computation.2 | async-start | bytes 5988352 | tf_op jit(solution)/shard_map/all_gather | solution.py:33
Sparse Core Ops, SparseCore 0:
  10.4 101.8 all-gather.5
  115.4 104.6 all-gather.11
  223.1 95.4 all-gather.7
  320.5 57.7 all-gather.9
where the time goes:
time: 475 us
  waiting for transfers between devices  338 us (71%)
  blocking collectives  73.8 us (16%)
  matrix products  34.7 us (7%)
  between operations  13.8 us (3%)
  local copies, waits for them, and re-layouts  12.8 us (3%)
    all_gather x1, waiting for transfers between devices, local(): full_act = lax.all_gather(activations, 'tensor', axis=1, tiled=True)  104 us
    all_gather x1, waiting for transfers between devices, local(): lax.all_gather(out_grads_t, 'tensor', axis=0, tiled=True)  101 us
    all_gather x1, waiting for transfers between devices, local(): act_proj = lax.all_gather(act_local, 'tensor', axis=1, tiled=True)  80.5 us
    psum x1, blocking collectives, local(): totals = lax.psum(partial_value, 'tensor')  73.8 us
    all_gather x1, waiting for transfers between devices, local(): lax.all_gather(scaled, 'dp', axis=2, tiled=True).astype(jnp.float32)  51.2 us
    dot_general x1, matrix products, local(): jnp.einsum('sij,qij->sq', projected, lax.all_gather(scaled, 'dp', axis=2,...  15.5 us
    unnamed x9, local copies, waits for them, and re-layouts  12.5 us
  transfers between devices with their start and end apart: 4, of which 4 were waited for; matrix products, arithmetic and copies ran while one was open for 7% of the time, Pallas kernels for 0%

commit v1 on v0

--- a/solution.py
+++ b/solution.py
@@ -2,6 +2,22 @@
 import jax.numpy as jnp
 from jax import lax
 from jax.sharding import PartitionSpec as P
+
+
+def collect(x, axis, dim):
+    ways, here, step = (lax.axis_size(axis), lax.axis_index(axis), x.shape[dim])
+    dims = [n * ways if d == dim else n for d, n in enumerate(x.shape)]
+    full = lax.dynamic_update_slice_in_dim(jnp.zeros(dims, x.dtype), x, here * step, axis=dim)
+    going_up = going_down = x
+    for far in range(1, ways // 2 + 1):
+        going_up = lax.ppermute(going_up, axis, [(d, (d + 1) % ways) for d in range(ways)])
+        full = lax.dynamic_update_slice_in_dim(full, going_up, (here - far) % ways * step, axis=dim)
+        if 2 * far < ways:
+            going_down = lax.ppermute(going_down, axis, [(d, (d - 1) % ways) for d in range(ways)])
+            full = lax.dynamic_update_slice_in_dim(
+                full, going_down, (here + far) % ways * step, axis=dim
+            )
+    return full
 
 
 def local(activations, out_grads_t, in_basis, out_basis_t, query_proj, eigvals, damping, lengths):
@@ -28,9 +44,7 @@
         preferred_element_type=jnp.float32,
     )
     partial_value = jnp.einsum(
-        "sij,qij->sq",
-        projected,
-        lax.all_gather(scaled, "dp", axis=2, tiled=True).astype(jnp.float32),
+        "sij,qij->sq", projected, collect(scaled, "dp", 2).astype(jnp.float32)
     )
     totals = lax.psum(partial_value, "tensor")
     norm_factor = (act_proj.shape[1] * out_basis_t.shape[1] * seq_len) ** (-0.5)

time: 475 us -> 425 us (0.89)
  waiting for transfers between devices: 338 us -> 251 us
  local copies, waits for them, and re-layouts: 12.8 us -> 34.5 us
  starting transfers between devices: 0.15 us -> 13.4 us
    all_gather x1, waiting for transfers between devices: 101 us -> 37.5 us  [local(): lax.all_gather(out_grads_t, 'tensor', axis=0, tiled=True)]
    all_gather x1 -> x0, waiting for transfers between devices: 51.2 us -> none  [local(): lax.all_gather(scaled, 'dp', axis=2, tiled=True).astype(jnp.float32)]
    ppermute x0 -> x15, waiting for transfers between devices: none -> 27.7 us  [the longest x8 26.2 us: collect(): lax.ppermute(going_up, axis, [(d, (d + 1) % ways) for d in range(ways)])]
    dynamic_update_slice x0 -> x15, local copies, waits for them, and re-layouts: none -> 16.4 us  [the longest x7 8.3 us: collect(): lax.dynamic_update_slice_in_dim(full, going_down, (here + far) % ways * s...]
    ppermute x0 -> x15, starting transfers between devices: none -> 13.4 us  [the longest x7 13.3 us: collect(): lax.ppermute(going_down, axis, [(d, (d - 1) % ways) for d in range(ways)])]
    broadcast_in_dim x0 -> x1, local copies, waits for them, and re-layouts: none -> 5.22 us  [collect(): jnp.zeros(dims, x.dtype)]
    unnamed x9 -> x13, local copies, waits for them, and re-layouts: 12.5 us -> 12.5 us
  transfers between devices with their start and end apart: 4 -> 18, of which waited for: 4 -> 13; matrix products, arithmetic and copies ran while one was open for 7% -> 11% of each run, Pallas kernels for 0% -> 0%
where the time goes in v1:
time: 425 us; the launch traced here: 424 us
  waiting for transfers between devices  251 us (59%)
  blocking collectives  74.5 us (18%)
  matrix products  34.7 us (8%)
  local copies, waits for them, and re-layouts  34.5 us (8%)
  between operations  14.1 us (3%)
  starting transfers between devices  13.4 us (3%)
    all_gather x1, waiting for transfers between devices, local(): full_act = lax.all_gather(activations, 'tensor', axis=1, tiled=True)  104 us
    all_gather x1, waiting for transfers between devices, local(): act_proj = lax.all_gather(act_local, 'tensor', axis=1, tiled=True)  80.5 us
    psum x1, blocking collectives, local(): totals = lax.psum(partial_value, 'tensor')  74.5 us
    all_gather x1, waiting for transfers between devices, local(): lax.all_gather(out_grads_t, 'tensor', axis=0, tiled=True)  37.5 us
    ppermute x8, waiting for transfers between devices, collect(): lax.ppermute(going_up, axis, [(d, (d + 1) % ways) for d in range(ways)])  26.2 us
    dot_general x1, matrix products, local(): jnp.einsum('sij,qij->sq', projected, collect(scaled, 'dp', 2).astype(jnp....  15.5 us
    ppermute x7, starting transfers between devices, collect(): lax.ppermute(going_down, axis, [(d, (d - 1) % ways) for d in range(ways)])  13.3 us
    unnamed x13, local copies, waits for them, and re-layouts  12.5 us
  transfers between devices with their start and end apart: 18, of which 13 were waited for; matrix products, arithmetic and copies ran while one was open for 11% of the time, Pallas kernels for 0%

profile of v1, /device:TPU:64, one launch (start us, length us, event | category | flops | bytes accessed | tf_op | source)
XLA Modules:
  0.0 424.2 jit_solution(1566481740816497662)
XLA Ops:
  8.1 104.2 %all-gather.5.cloned.1.call-done = bf16[768,4096]{1,0:T(8,128)(2,1)} async-done(((bf16[768,128]{1,0:T(8,128)(2,1)}), bf16[768,4096]{1,0:T(8,128)(2,1)}) %all-gather.5.cloned.1.call-update) | async-done | bytes 6291472 | tf_op jit(solution)/shard_map/all_gather | solution.py:24
  112.3 5.5 %convolution_convert_fusion = bf16[768,128]{1,0:T(8,128)(2,1)} fusion(bf16[768,4096]{1,0:T(8,128)(2,1)} %all-gather.5.cloned.1.call-done, bf16[4096,128]{1,0:T(8,128)(2,1)} %param.10), kind=kOutput, calls=%fused_computation.4 | convolution fusion | flops 805404672 | bytes 7536640 | tf_op jit(solution)/shard_map/dot_general | solution.py:25
  118.5 5.2 %broadcast_in_dim.2 = bf16[4,172,4096]{2,0,1:T(4,128)(2,1)} broadcast(bf16[]{:T(256)} %constant.91.clone.1), dimensions={} | broadcast | bytes 5636098 | tf_op jit(solution)/shard_map/broadcast_in_dim | solution.py:10
  123.7 1.0 constant_dynamic-update-slice_fusion.15
  124.7 1.7 collective-permute-start.1
  126.5 5.0 %collective-permute-done = bf16[4,172,256]{2,0,1:T(4,128)(2,1)S(1)} collective-permute-done((bf16[4,172,256]{2,0,1:T(4,128)(2,1)S(1)}, bf16[4,172,256]{2,0,1:T(4,128)(2,1)S(1)}, u32[]{:S(2)}, u32[]{:S(2)}) %collective-permute-start) | collective-permute-done | bytes 352288 | tf_op jit(solution)/shard_map/ppermute | solution.py:13
  131.5 1.7 collective-permute-start.3
  133.2 5.0 %collective-permute-done.2 = bf16[4,172,256]{2,0,1:T(4,128)(2,1)S(1)} collective-permute-done((bf16[4,172,256]{2,0,1:T(4,128)(2,1)S(1)}, bf16[4,172,256]{2,0,1:T(4,128)(2,1)S(1)}, u32[]{:S(2)}, u32[]{:S(2)}) %collective-permute-start.2) | collective-permute-done | bytes 352288 | tf_op jit(solution)/shard_map/ppermute | solution.py:13
  138.3 2.1 collective-permute-start.5
  140.4 4.6 %collective-permute-done.4 = bf16[4,172,256]{2,0,1:T(4,128)(2,1)S(1)} collective-permute-done((bf16[4,172,256]{2,0,1:T(4,128)(2,1)S(1)}, bf16[4,172,256]{2,0,1:T(4,128)(2,1)S(1)}, u32[]{:S(2)}, u32[]{:S(2)}) %collective-permute-start.4) | collective-permute-done | bytes 352288 | tf_op jit(solution)/shard_map/ppermute | solution.py:13
  145.3 1.9 constant_dynamic-update-slice_fusion.14
  147.2 1.5 collective-permute-start.7
  148.7 1.9 constant_dynamic-update-slice_fusion.13
  150.6 1.2 collective-permute-done.6
  152.7 1.9 constant_dynamic-update-slice_fusion.11
  154.5 1.8 collective-permute-start.9
  157.2 1.4 collective-permute-done.8
  161.2 2.2 collective-permute-start.11
  164.3 1.5 collective-permute-done.10
  168.2 2.2 collective-permute-start.13
  171.3 2.3 collective-permute-done.12
  173.6 0.9 constant_dynamic-update-slice_fusion.3
  174.5 0.9 constant_dynamic-update-slice_fusion.2
  175.4 0.9 constant_dynamic-update-slice_fusion.1
  176.3 5.2 %collective-permute-done.14 = bf16[4,172,256]{2,0,1:T(4,128)(2,1)S(1)} collective-permute-done((bf16[4,172,256]{2,0,1:T(4,128)(2,1)S(1)}, bf16[4,172,256]{2,0,1:T(4,128)(2,1)S(1)}, u32[]{:S(2)}, u32[]{:S(2)}) %collective-permute-start.14) | collective-permute-done | bytes 352288 | tf_op jit(solution)/shard_map/ppermute | solution.py:13
  182.5 37.5 %all-gather.9.cloned.1.call-done = bf16[32,172,768]{2,1,0:T(8,128)(2,1)} async-done(((bf16[1,172,768]{2,1,0:T(8,128)(2,1)}), bf16[32,172,768]{2,1,0:T(8,128)(2,1)}) %all-gather.9.cloned.1.call-update) | async-done | bytes 8454160 | tf_op jit(solution)/shard_map/all_gather | solution.py:31
  220.0 12.5 %reshape.30 = bf16[5504,768]{1,0:T(8,128)(2,1)} reshape(bf16[32,172,768]{2,1,0:T(8,128)(2,1)} %all-gather.9.cloned.1.call-done) | data formatting | bytes 16908288
  232.5 5.2 %fusion.2 = bf16[172,768]{1,0:T(8,128)(2,1)S(1)} fusion(bf16[172,5504]{1,0:T(8,128)(2,1)S(1)} %copy-done, bf16[5504,768]{1,0:T(8,128)(2,1)} %reshape.30, f32[768]{0:T(1024)S(1)} %convert_bitcast_fusion), kind=kOutput, calls=%fused_computation.3 | convolution fusion | flops 1454376960 | bytes 10614784 | tf_op jit(solution)/shard_map/dot_general | solution.py:29
  238.0 80.5 %all-gather.7.cloned.1.call-done = bf16[768,4096]{1,0:T(8,128)(2,1)} async-done(((bf16[768,128]{1,0:T(8,128)(2,1)}), bf16[768,4096]{1,0:T(8,128)(2,1)}) %all-gather.7.cloned.1.call-update) | async-done | bytes 6291472 | tf_op jit(solution)/shard_map/all_gather | solution.py:26
  318.5 8.5 %fusion.7 = bf16[6,172,4096]{2,1,0:T(8,128)(2,1)} fusion(bf16[6,128,4096]{2,1,0:T(8,128)(2,1)} %bitcast.14, bf16[172,6,128]{2,1,0:T(8,128)(2,1)S(1)} %reshape.26), kind=kOutput, calls=%fused_computation.8 | convolution fusion | flops 1082130432 | bytes 15009792 | tf_op jit(solution)/shard_map/jst,std->sjd/dot_general | solution.py:40
  327.0 15.5 %fusion.3 = f32[6,4]{0,1:T(4,128)S(1)} fusion(bf16[4,172,4096]{2,0,1:T(4,128)(2,1)} %constant_dynamic-update-slice_fusion, bf16[6,172,4096]{2,1,0:T(8,128)(2,1)} %fusion.7), kind=kOutput, calls=%fused_computation.5 | convolution fusion | flops 33816576 | bytes 14090336 | tf_op jit(solution)/shard_map/sij,qij->sq/dot_general | solution.py:46
  342.6 74.5 %psum.7 = f32[6,4]{0,1:T(4,128)S(1)} all-reduce(f32[6,4]{0,1:T(4,128)S(1)} %fusion.3), channel_id=1, replica_groups=mesh['dp'=16,'tensor'=32] {'tensor'}, use_global_device_ids=true, to_apply=%region_0.1 | all-reduce | flops 24 | bytes 192 | tf_op jit(solution)/shard_map/psum | solution.py:49
  (46 shorter events, 12.0 us)
Async XLA Ops:
  6.5 225.9 %copy-start = (bf16[172,5504]{1,0:T(8,128)(2,1)S(1)}, bf16[172,5504]{1,0:T(8,128)(2,1)}, u32[]{:S(2)}) copy-start(bf16[172,5504]{1,0:T(8,128)(2,1)} %param.11) | copy-start | bytes 5680132
  6.5 111.9 %copy-start.4 = (f32[172,256]{1,0:T(8,128)S(1)}, f32[172,256]{1,0:T(8,128)}, u32[]{:S(2)}) copy-start(f32[172,256]{1,0:T(8,128)} %param.13) | copy-start | bytes 528388
  6.5 105.7 %all-gather.5.cloned.1.call-start = ((), (), s32[]{:S(2)}) async-start(), calls=%async_computation | async-start | bytes 6488064 | tf_op jit(solution)/shard_map/all_gather | solution.py:24
  7.3 212.7 %all-gather.9.cloned.1.call-start = ((), (), s32[]{:S(2)}) async-start(), calls=%async_computation.2 | async-start | bytes 8921088 | tf_op jit(solution)/shard_map/all_gather | solution.py:31
  8.0 115.7 %copy-start.3 = (bf16[4,172,256]{2,0,1:T(4,128)(2,1)S(1)}, bf16[4,172,256]{2,0,1:T(4,128)(2,1)}, u32[]{:S(2)}) copy-start(bf16[4,172,256]{2,0,1:T(4,128)(2,1)} %param.12) | copy-start | bytes 1056772
  8.0 310.5 %all-gather.7.cloned.1.call-start = ((), (), s32[]{:S(2)}) async-start(), calls=%async_computation.1 | async-start | bytes 6488064 | tf_op jit(solution)/shard_map/all_gather | solution.py:26
  117.8 27.3 %copy-start.5 = (s32[6]{0:T(128)S(1)}, s32[6]{0:T(128)}, u32[]{:S(2)}) copy-start(s32[6]{0:T(128)} %param.15) | copy-start | bytes 76
  124.7 6.8 %collective-permute-start = (bf16[4,172,256]{2,0,1:T(4,128)(2,1)S(1)}, bf16[4,172,256]{2,0,1:T(4,128)(2,1)S(1)}, u32[]{:S(2)}, u32[]{:S(2)}) collective-permute-start(bf16[4,172,256]{2,0,1:T(4,128)(2,1)S(1)} %get-tuple-element.6), channel_id=1, source_target_pairs={{0,32},{32,64},{64,96},{96,128},{128,160},{160,192},{192,224},{224... | collective-permute-start | bytes 1056776 | tf_op jit(solution)/shard_map/ppermute | solution.py:13
  124.7 6.8 %collective-permute-start.1 = (bf16[4,172,256]{2,0,1:T(4,128)(2,1)S(1)}, bf16[4,172,256]{2,0,1:T(4,128)(2,1)S(1)}, u32[]{:S(2)}, u32[]{:S(2)}) collective-permute-start(bf16[4,172,256]{2,0,1:T(4,128)(2,1)S(1)} %get-tuple-element.6), channel_id=1, source_target_pairs={{0,480},{32,0},{64,32},{96,64},{128,96},{160,128},{192,160},{224,1... | collective-permute-start | bytes 1056776 | tf_op jit(solution)/shard_map/ppermute | solution.py:16
  131.5 8.9 %copy-start.2 = (bf16[4,172,256]{2,0,1:T(4,128)(2,1)}, bf16[4,172,256]{2,0,1:T(4,128)(2,1)S(1)}, u32[]{:S(2)}) copy-start(bf16[4,172,256]{2,0,1:T(4,128)(2,1)S(1)} %collective-permute-done) | copy-start | bytes 1056772
  131.5 6.8 %collective-permute-start.2 = (bf16[4,172,256]{2,0,1:T(4,128)(2,1)S(1)}, bf16[4,172,256]{2,0,1:T(4,128)(2,1)S(1)}, u32[]{:S(2)}, u32[]{:S(2)}) collective-permute-start(bf16[4,172,256]{2,0,1:T(4,128)(2,1)S(1)} %collective-permute-done), channel_id=1, source_target_pairs={{0,32},{32,64},{64,96},{96,128},{128,160},{160,192},{192,224},{224... | collective-permute-start | bytes 1056776 | tf_op jit(solution)/shard_map/ppermute | solution.py:13
  131.5 6.8 %copy-start.1 = (bf16[4,172,256]{2,0,1:T(4,128)(2,1)}, bf16[4,172,256]{2,0,1:T(4,128)(2,1)S(1)}, u32[]{:S(2)}) copy-start(bf16[4,172,256]{2,0,1:T(4,128)(2,1)S(1)} %collective-permute-done.1) | copy-start | bytes 1056772
  131.5 6.8 %collective-permute-start.3 = (bf16[4,172,256]{2,0,1:T(4,128)(2,1)S(1)}, bf16[4,172,256]{2,0,1:T(4,128)(2,1)}, u32[]{:S(2)}, u32[]{:S(2)}) collective-permute-start(bf16[4,172,256]{2,0,1:T(4,128)(2,1)S(1)} %collective-permute-done.1), channel_id=1, source_target_pairs={{0,480},{32,0},{64,32},{96,64},{128,96},{160,128},{192,160},{224,1... | collective-permute-start | bytes 1056776 | tf_op jit(solution)/shard_map/ppermute | solution.py:16
  138.2 6.8 %collective-permute-start.4 = (bf16[4,172,256]{2,0,1:T(4,128)(2,1)S(1)}, bf16[4,172,256]{2,0,1:T(4,128)(2,1)S(1)}, u32[]{:S(2)}, u32[]{:S(2)}) collective-permute-start(bf16[4,172,256]{2,0,1:T(4,128)(2,1)S(1)} %collective-permute-done.2), channel_id=1, source_target_pairs={{0,32},{32,64},{64,96},{96,128},{128,160},{160,192},{192,224},{224... | collective-permute-start | bytes 1056776 | tf_op jit(solution)/shard_map/ppermute | solution.py:13
  138.3 8.9 %collective-permute-start.5 = (bf16[4,172,256]{2,0,1:T(4,128)(2,1)}, bf16[4,172,256]{2,0,1:T(4,128)(2,1)S(1)}, u32[]{:S(2)}, u32[]{:S(2)}) collective-permute-start(bf16[4,172,256]{2,0,1:T(4,128)(2,1)} %collective-permute-done.3), channel_id=1, source_target_pairs={{0,480},{32,0},{64,32},{96,64},{128,96},{160,128},{192,160},{224,1... | collective-permute-start | bytes 1056776 | tf_op jit(solution)/shard_map/ppermute | solution.py:16
  145.0 6.8 %collective-permute-start.6 = (bf16[4,172,256]{2,0,1:T(4,128)(2,1)S(1)}, bf16[4,172,256]{2,0,1:T(4,128)(2,1)S(1)}, u32[]{:S(2)}, u32[]{:S(2)}) collective-permute-start(bf16[4,172,256]{2,0,1:T(4,128)(2,1)S(1)} %collective-permute-done.4), channel_id=1, source_target_pairs={{0,32},{32,64},{64,96},{96,128},{128,160},{160,192},{192,224},{224... | collective-permute-start | bytes 1056776 | tf_op jit(solution)/shard_map/ppermute | solution.py:13
  147.2 7.4 %collective-permute-start.7 = (bf16[4,172,256]{2,0,1:T(4,128)(2,1)S(1)}, bf16[4,172,256]{2,0,1:T(4,128)(2,1)S(1)}, u32[]{:S(2)}, u32[]{:S(2)}) collective-permute-start(bf16[4,172,256]{2,0,1:T(4,128)(2,1)S(1)} %collective-permute-done.5), channel_id=1, source_target_pairs={{0,480},{32,0},{64,32},{96,64},{128,96},{160,128},{192,160},{224,1... | collective-permute-start | bytes 1056776 | tf_op jit(solution)/shard_map/ppermute | solution.py:16
  151.8 6.8 %collective-permute-start.8 = (bf16[4,172,256]{2,0,1:T(4,128)(2,1)S(1)}, bf16[4,172,256]{2,0,1:T(4,128)(2,1)S(1)}, u32[]{:S(2)}, u32[]{:S(2)}) collective-permute-start(bf16[4,172,256]{2,0,1:T(4,128)(2,1)S(1)} %collective-permute-done.6), channel_id=1, source_target_pairs={{0,32},{32,64},{64,96},{96,128},{128,160},{160,192},{192,224},{224... | collective-permute-start | bytes 1056776 | tf_op jit(solution)/shard_map/ppermute | solution.py:13
  154.5 6.6 %collective-permute-start.9 = (bf16[4,172,256]{2,0,1:T(4,128)(2,1)S(1)}, bf16[4,172,256]{2,0,1:T(4,128)(2,1)S(1)}, u32[]{:S(2)}, u32[]{:S(2)}) collective-permute-start(bf16[4,172,256]{2,0,1:T(4,128)(2,1)S(1)} %collective-permute-done.7), channel_id=1, source_target_pairs={{0,480},{32,0},{64,32},{96,64},{128,96},{160,128},{192,160},{224,1... | collective-permute-start | bytes 1056776 | tf_op jit(solution)/shard_map/ppermute | solution.py:16
  158.5 7.3 %collective-permute-start.10 = (bf16[4,172,256]{2,0,1:T(4,128)(2,1)S(1)}, bf16[4,172,256]{2,0,1:T(4,128)(2,1)S(1)}, u32[]{:S(2)}, u32[]{:S(2)}) collective-permute-start(bf16[4,172,256]{2,0,1:T(4,128)(2,1)S(1)} %collective-permute-done.8), channel_id=1, source_target_pairs={{0,32},{32,64},{64,96},{96,128},{128,160},{160,192},{192,224},{224... | collective-permute-start | bytes 1056776 | tf_op jit(solution)/shard_map/ppermute | solution.py:13
  161.2 7.1 %collective-permute-start.11 = (bf16[4,172,256]{2,0,1:T(4,128)(2,1)S(1)}, bf16[4,172,256]{2,0,1:T(4,128)(2,1)S(1)}, u32[]{:S(2)}, u32[]{:S(2)}) collective-permute-start(bf16[4,172,256]{2,0,1:T(4,128)(2,1)S(1)} %collective-permute-done.9), channel_id=1, source_target_pairs={{0,480},{32,0},{64,32},{96,64},{128,96},{160,128},{192,160},{224,1... | collective-permute-start | bytes 1056776 | tf_op jit(solution)/shard_map/ppermute | solution.py:16
  165.8 7.8 %collective-permute-start.12 = (bf16[4,172,256]{2,0,1:T(4,128)(2,1)S(1)}, bf16[4,172,256]{2,0,1:T(4,128)(2,1)S(1)}, u32[]{:S(2)}, u32[]{:S(2)}) collective-permute-start(bf16[4,172,256]{2,0,1:T(4,128)(2,1)S(1)} %collective-permute-done.10), channel_id=1, source_target_pairs={{0,32},{32,64},{64,96},{96,128},{128,160},{160,192},{192,224},{224... | collective-permute-start | bytes 1056776 | tf_op jit(solution)/shard_map/ppermute | solution.py:13
  168.2 7.2 %collective-permute-start.13 = (bf16[4,172,256]{2,0,1:T(4,128)(2,1)S(1)}, bf16[4,172,256]{2,0,1:T(4,128)(2,1)S(1)}, u32[]{:S(2)}, u32[]{:S(2)}) collective-permute-start(bf16[4,172,256]{2,0,1:T(4,128)(2,1)S(1)} %collective-permute-done.11), channel_id=1, source_target_pairs={{0,480},{32,0},{64,32},{96,64},{128,96},{160,128},{192,160},{224,1... | collective-permute-start | bytes 1056776 | tf_op jit(solution)/shard_map/ppermute | solution.py:16
  173.6 8.0 %collective-permute-start.14 = (bf16[4,172,256]{2,0,1:T(4,128)(2,1)S(1)}, bf16[4,172,256]{2,0,1:T(4,128)(2,1)S(1)}, u32[]{:S(2)}, u32[]{:S(2)}) collective-permute-start(bf16[4,172,256]{2,0,1:T(4,128)(2,1)S(1)} %collective-permute-done.12), channel_id=1, source_target_pairs={{0,32},{32,64},{64,96},{96,128},{128,160},{160,192},{192,224},{224... | collective-permute-start | bytes 1056776 | tf_op jit(solution)/shard_map/ppermute | solution.py:13
Sparse Core Ops, SparseCore 0:
  10.4 101.8 all-gather.4
  115.4 104.5 all-gather.8
  223.0 95.4 all-gather.6
